TPU v7x, 512 devices: a whole 4x8x8 slice. The times are simulated.
512 devices in a mesh: grp: 16 (over y, core), seq: 32 (over z, x).
Axes of the slice: x: 4, y: 8, z: 8, core: 2. Of those that a mesh axis runs over, the one named last changes fastest.
Arguments:
- queries: bfloat16 [16, 4096, 4096], P('grp', 'seq'), may hold values from -6 to 6
- keys_values: bfloat16 [16, 4096, 1024], P('grp', 'seq'), may hold values from -6 to 6
- route_group: int32 [16, 4096], P('grp', 'seq'), may hold values from 0 to 15, as said below
- route_slot: int32 [16, 4096], P('grp', 'seq'), may hold values from 0 to 127, as said below
- doc_lengths: int32 [16, 2, 3], P('grp'), may hold values from 1 to 1024, 2048 in all within a row
Outputs:
- attn_out: bfloat16 [16, 4096, 4096], P('grp', 'seq')
Inputs may be any that keep to these rules, and one draw needn't show every extreme that they name: `route_group`: A row keeps its position index s along seq. For each s, every packed row receives exactly 128 rows in all; from one generator device at most 16 rows go to one packed row, and for every s and every packed row exactly one generator device sends exactly 16. `route_slot`: the rows that reach one device (same packed row, same s) have distinct places.
All inputs are finite; a program needn't handle non-finite values.
Results may differ from a plain program's by a relative error of at most 0.004.
Values may be sent and summed in bfloat16 or wider, within the bound.
A program may use at most 128 MiB of HBM per device.

v0:
```python
import functools
import math

import jax
import jax.numpy as jnp
from jax import lax
from jax.experimental import pallas as pl
from jax.experimental.pallas import tpu as pltpu
from jax.sharding import PartitionSpec as P

HQ = 32
HK = 4
HD = 128
TOK = 128
GROUPS = 16
CAP = 16
SLOTS = GROUPS * CAP
WIDE = HQ // HK * HD
PAIR = 2 * HK * HD
BACK = 8
SPAN = (BACK + 1) * TOK
NX = 4
HALF_ROWS = 4
NEGATIVE = -1e30
MESH = pl.DeviceIdType.MESH
FACTOR = HD ** (-0.5) * math.log2(math.e)


def remote(src, dst, send, recv, device):
    return pltpu.make_async_remote_copy(
        src_ref=src,
        dst_ref=dst,
        send_sem=send,
        recv_sem=recv,
        device_id=device,
        device_id_type=MESH,
    )


def contract(a, b, dims):
    return lax.dot_general(a, b, (dims, ((), ())), preferred_element_type=jnp.float32)


def kernel(
    q_hbm,
    kv_ref,
    group_ref,
    slot_ref,
    length_ref,
    out_hbm,
    q_in,
    q_send,
    q_recv,
    kv_send,
    kv_recv,
    window,
    mask,
    placed,
    out_buf,
    in_sem,
    out_sem,
    q_ss,
    q_rs,
    kv_ss,
    kv_rs,
    z_ss,
    z_rs,
    x_ss,
    x_rs,
):
    me = lax.axis_index("grp")
    seq = lax.axis_index("seq")
    z = seq // NX
    x = seq % NX
    zz = z % HALF_ROWS
    has_next = zz < HALF_ROWS - 1
    has_last = zz > 0

    def load(j):
        cols = pl.ds(j * WIDE, WIDE)
        return pltpu.make_async_copy(q_hbm.at[0, :, cols], q_in.at[:, cols], in_sem.at[j])

    for j in range(HK):
        load(j).start()

    barrier = pltpu.get_barrier_semaphore()

    def greet(group, place):
        pl.semaphore_signal(barrier, inc=1, device_id=(group, place), device_id_type=MESH)

    for d in range(1, GROUPS):
        greet((me + d) % GROUPS, seq)
    for d in range(1, NX):
        greet(me, z * NX + (x + d) % NX)

    @pl.when(has_next)
    def _():
        greet(me, seq + NX)

    @pl.when(has_last)
    def _():
        greet(me, seq - NX)

    targets = group_ref[...]
    lane = lax.broadcasted_iota(jnp.int32, (TOK, TOK), 1)
    sub = lax.broadcasted_iota(jnp.int32, (TOK, TOK), 0)
    hits = lax.broadcasted_iota(jnp.int32, (GROUPS, TOK), 0) == targets
    before = (sub < lane).astype(jnp.float32).astype(jnp.bfloat16)
    hits_f = hits.astype(jnp.float32)
    ranks = contract(hits_f.astype(jnp.bfloat16), before, ((1,), (0,)))
    ranks = jnp.where(hits, ranks, -1.0)
    level = lax.broadcasted_iota(jnp.int32, (GROUPS, CAP, TOK), 1).astype(jnp.float32)
    pick_f = (ranks[:, None, :] == level).astype(jnp.float32).reshape(SLOTS, TOK)
    pick = pick_f.astype(jnp.bfloat16)
    marks = (pick_f * (slot_ref[...] + 1).astype(jnp.float32)).astype(jnp.bfloat16)
    slots = contract(marks, jnp.ones((TOK, TOK), jnp.bfloat16), ((1,), (0,)))
    kv_send[:, :, PAIR:] = slots.astype(jnp.bfloat16).reshape(GROUPS, CAP, TOK)
    kv_send[:, :, :PAIR] = (
        contract(pick, kv_ref[0], ((1,), (0,))).astype(jnp.bfloat16).reshape(GROUPS, CAP, PAIR)
    )

    pl.semaphore_wait(
        barrier, GROUPS - 1 + NX - 1 + has_next.astype(jnp.int32) + has_last.astype(jnp.int32)
    )

    def kv_copy(d):
        target = (me + d) % GROUPS
        return remote(
            kv_send.at[target], kv_recv.at[me], kv_ss.at[d], kv_rs.at[d], (target, seq)
        )

    @pl.loop(1, GROUPS)
    def _(d):
        kv_copy(d).start()

    kv_recv[me] = kv_send[me]

    def q_copy(j, d):
        target = (me + d) % GROUPS
        return remote(
            q_send.at[j, target], q_recv.at[j, me], q_ss.at[j, d], q_rs.at[j, d], (target, seq)
        )

    for j in range(HK):
        load(j).wait()
        q_send[j] = (
            contract(pick, q_in[:, j * WIDE : (j + 1) * WIDE], ((1,), (0,)))
            .astype(jnp.bfloat16)
            .reshape(GROUPS, CAP, WIDE)
        )

        @pl.loop(1, GROUPS)
        def _(d, j=j):
            q_copy(j, d).start()

        q_recv[j, me] = q_send[j, me]

    query = seq * TOK + lax.broadcasted_iota(jnp.int32, (TOK, SPAN), 0)
    key = (seq - BACK) * TOK + lax.broadcasted_iota(jnp.int32, (TOK, SPAN), 1)
    begin = jnp.zeros((TOK, SPAN), jnp.int32)
    bound = jnp.int32(0)
    for half in range(2):
        for n in range(3):
            bound = bound + length_ref[0, half, n]
            begin = jnp.where(query >= bound, bound, begin)
    mask[...] = jnp.where((key >= begin) & (key <= query), 0.0, NEGATIVE)

    @pl.when(zz == 0)
    def _():
        window[pl.ds(0, 2 * NX)] = jnp.zeros((2 * NX, TOK, PAIR), jnp.bfloat16)

    @pl.when(zz == 1)
    def _():
        window[pl.ds(0, NX)] = jnp.zeros((NX, TOK, PAIR), jnp.bfloat16)

    @pl.loop(1, GROUPS)
    def _(d):
        kv_copy(d).wait_recv()

    marks_in = kv_recv[:, :, PAIR:].reshape(SLOTS, TOK).astype(jnp.float32)
    column = lax.broadcasted_iota(jnp.int32, (SLOTS, TOK), 1).astype(jnp.float32) + 1.0
    put = (marks_in == column).astype(jnp.float32).T.astype(jnp.bfloat16)
    window[2 * NX + x] = contract(
        put, kv_recv[:, :, :PAIR].reshape(SLOTS, PAIR), ((1,), (0,))
    ).astype(jnp.bfloat16)

    def z_copy(plane):
        return remote(
            window.at[plane * NX + x],
            window.at[(plane - 1) * NX + x],
            z_ss.at[plane],
            z_rs.at[plane],
            (me, (seq + NX) % (NX * 8)),
        )

    def x_copy(plane, d):
        return remote(
            window.at[plane * NX + x],
            window.at[plane * NX + x],
            x_ss.at[plane, d],
            x_rs.at[plane, d],
            (me, z * NX + (x + d) % NX),
        )

    def x_wait(plane, d):
        source = (x + NX - d) % NX
        return remote(
            window.at[plane * NX + source],
            window.at[plane * NX + source],
            x_ss.at[plane, d],
            x_rs.at[plane, d],
            (me, z * NX + (x + d) % NX),
        )

    def each_x(plane, act, sending):
        for d in range(1, NX):
            wraps = x + d >= NX if sending else x - d < 0
            if plane == 1:
                act(plane, d)
            else:
                pl.when(wraps if plane == 0 else jnp.logical_not(wraps))(
                    functools.partial(act, plane, d)
                )

    def start_x(plane, d):
        x_copy(plane, d).start()

    def sent_x(plane, d):
        x_copy(plane, d).wait_send()

    def came_x(plane, d):
        x_wait(plane, d).wait_recv()

    @pl.when(has_next)
    def _():
        z_copy(2).start()

    each_x(2, start_x, True)

    @pl.when(has_last)
    def _():
        z_copy(2).wait_recv()

        @pl.when(has_next)
        def _():
            z_copy(1).start()

        each_x(1, start_x, True)

    @pl.when(zz >= 2)
    def _():
        z_copy(1).wait_recv()
        each_x(0, start_x, True)

    each_x(2, came_x, False)

    @pl.when(has_last)
    def _():
        each_x(1, came_x, False)

    @pl.when(zz >= 2)
    def _():
        each_x(0, came_x, False)

    def store(j):
        cols = pl.ds(pl.multiple_of(j * WIDE, WIDE), WIDE)
        return pltpu.make_async_copy(out_buf.at[:, cols], out_hbm.at[0, :, cols], out_sem.at[j])

    @pl.loop(0, HK)
    def _(j):
        @pl.loop(1, GROUPS)
        def _(d):
            q_copy(j, d).wait_recv()

        rows = contract(put, q_recv[j].reshape(SLOTS, WIDE), ((1,), (0,))).astype(jnp.bfloat16)
        for h in range(HQ // HK):
            placed[h] = rows[:, h * HD : (h + 1) * HD]
        key_cols = pl.ds(pl.multiple_of(j * HD, HD), HD)
        value_cols = pl.ds(pl.multiple_of((HK + j) * HD, HD), HD)

        @pl.loop(0, HQ // HK)
        def _(h):
            keys = window[pl.ds(x, BACK + 1), :, key_cols].reshape(SPAN, HD)
            values = window[pl.ds(x, BACK + 1), :, value_cols].reshape(SPAN, HD)
            scores = contract(placed[h], keys, ((1,), (1,))) + mask[...]
            top = jnp.max(scores, axis=1, keepdims=True)
            raised = jnp.exp2((scores - top) * FACTOR)
            total = jnp.sum(raised, axis=1, keepdims=True)
            summed = contract(raised.astype(jnp.bfloat16), values, ((1,), (0,)))
            cols = pl.ds(pl.multiple_of((j * (HQ // HK) + h) * HD, HD), HD)
            out_buf[:, cols] = (summed / total).astype(jnp.bfloat16)

        store(j).start()

    for j in range(HK):
        store(j).wait()

    @pl.loop(1, GROUPS)
    def _(d):
        kv_copy(d).wait_send()
        for j in range(HK):
            q_copy(j, d).wait_send()

    each_x(2, sent_x, True)

    @pl.when(has_next)
    def _():
        z_copy(2).wait_send()

    @pl.when(has_last)
    def _():
        each_x(1, sent_x, True)

        @pl.when(has_next)
        def _():
            z_copy(1).wait_send()

    @pl.when(zz >= 2)
    def _():
        each_x(0, sent_x, True)


def local(queries, keys_values, route_group, route_slot, doc_lengths):
    bf16 = jnp.bfloat16
    dma = pltpu.SemaphoreType.DMA
    return pl.pallas_call(
        kernel,
        out_shape=jax.ShapeDtypeStruct((1, TOK, HQ * HD), bf16),
        in_specs=[
            pl.BlockSpec(memory_space=pl.ANY),
            pl.BlockSpec(memory_space=pltpu.VMEM),
            pl.BlockSpec(memory_space=pltpu.VMEM),
            pl.BlockSpec(memory_space=pltpu.VMEM),
            pl.BlockSpec(memory_space=pltpu.SMEM),
        ],
        out_specs=pl.BlockSpec(memory_space=pl.ANY),
        scratch_shapes=[
            pltpu.VMEM((TOK, HQ * HD), bf16),
            pltpu.VMEM((HK, GROUPS, CAP, WIDE), bf16),
            pltpu.VMEM((HK, GROUPS, CAP, WIDE), bf16),
            pltpu.VMEM((GROUPS, CAP, PAIR + TOK), bf16),
            pltpu.VMEM((GROUPS, CAP, PAIR + TOK), bf16),
            pltpu.VMEM((3 * NX, TOK, PAIR), bf16),
            pltpu.VMEM((TOK, SPAN), jnp.float32),
            pltpu.VMEM((HQ // HK, TOK, HD), bf16),
            pltpu.VMEM((TOK, HQ * HD), bf16),
            dma((HK,)),
            dma((HK,)),
            dma((HK, GROUPS)),
            dma((HK, GROUPS)),
            dma((GROUPS,)),
            dma((GROUPS,)),
            dma((3,)),
            dma((3,)),
            dma((3, NX)),
            dma((3, NX)),
        ],
        compiler_params=pltpu.CompilerParams(
            collective_id=0, has_side_effects=True, vmem_limit_bytes=48 << 20
        ),
    )(queries, keys_values, route_group, route_slot, doc_lengths)


def solution(mesh):
    return jax.shard_map(
        local,
        mesh=mesh,
        in_specs=(
            P("grp", "seq", None),
            P("grp", "seq", None),
            P("grp", "seq"),
            P("grp", "seq"),
            P("grp", None, None),
        ),
        out_specs=P("grp", "seq", None),
        check_vma=False,
    )
```

profile of v0, /device:TPU:1, one launch (start us, length us, event | category | flops | bytes accessed | tf_op | source)
XLA Modules:
  0.0 84.5 jit_solution(16117275437520989232)
XLA Ops:
  0.0 0.0 copy-start
  0.0 1.2 %copy-done = bf16[1,128,4096]{2,1,0:T(8,128)(2,1)S(1)} copy-done((bf16[1,128,4096]{2,1,0:T(8,128)(2,1)S(1)}, bf16[1,128,4096]{2,1,0:T(8,128)(2,1)}, u32[]{:S(2)}) %copy-start) | copy-done | bytes 1048600
  1.2 0.0 copy-start.1
  1.2 0.9 %copy-done.1 = bf16[1,128,1024]{2,1,0:T(8,128)(2,1)S(1)} copy-done((bf16[1,128,1024]{2,1,0:T(8,128)(2,1)S(1)}, bf16[1,128,1024]{2,1,0:T(8,128)(2,1)}, u32[]{:S(2)}) %copy-start.1) | copy-done | bytes 262168
  2.2 0.0 copy-start.2
  2.2 0.7 copy-done.2
  2.9 0.0 copy-start.3
  2.9 0.7 copy-done.3
  3.5 0.0 copy-start.4
  3.5 0.7 copy-done.4
  4.2 79.3 %shard_map.55 = bf16[1,128,4096]{2,1,0:T(8,128)(2,1)S(1)} custom-call(bf16[1,128,4096]{2,1,0:T(8,128)(2,1)S(1)} %copy-done, bf16[1,128,1024]{2,1,0:T(8,128)(2,1)S(1)} %copy-done.1, s32[1,128]{1,0:T(1,128)S(1)} %copy-done.3, s32[1,128]{1,0:T(1,128)S(1)} %copy-done.4, s32[1,2,3]{2,1,0:T(2,128)S(1)} %copy-done.2), custom_call_target="tpu_custom_call" | custom-call | tf_op jit(solution)/shard_map/pallas_call | solution.py:326
  83.5 1.0 %copy.7 = bf16[1,128,4096]{2,1,0:T(8,128)(2,1)} copy(bf16[1,128,4096]{2,1,0:T(8,128)(2,1)S(1)} %shard_map.55) | data formatting | bytes 2097152
Async XLA Ops:
  0.0 1.2 %copy-start = (bf16[1,128,4096]{2,1,0:T(8,128)(2,1)S(1)}, bf16[1,128,4096]{2,1,0:T(8,128)(2,1)}, u32[]{:S(2)}) copy-start(bf16[1,128,4096]{2,1,0:T(8,128)(2,1)} %q_hbm.1) | copy-start | bytes 3145732
  1.2 0.9 %copy-start.1 = (bf16[1,128,1024]{2,1,0:T(8,128)(2,1)S(1)}, bf16[1,128,1024]{2,1,0:T(8,128)(2,1)}, u32[]{:S(2)}) copy-start(bf16[1,128,1024]{2,1,0:T(8,128)(2,1)} %kv_ref.1) | copy-start | bytes 786436
  2.2 0.7 copy-start.2
  2.9 0.7 copy-start.3
  3.5 0.7 copy-start.4
where the time goes:
time: 85.1 us; the launch traced here: 84.5 us
  Pallas kernels  79.3 us (93%)
  local copies, waits for them, and re-layouts  5.13 us (6%)
    pallas_call x1, Pallas kernels, local(): pl.pallas_call(kernel, out_shape=jax.ShapeDtypeStruct((1, TOK, HQ * HD),...  79.3 us
    unnamed x11, local copies, waits for them, and re-layouts  5.13 us

commit v1 on v0

--- a/solution.py
+++ b/solution.py
@@ -43,12 +43,16 @@
 
 def kernel(
     q_hbm,
+    kv_hbm,
+    group_hbm,
+    slot_hbm,
+    length_hbm,
+    out_hbm,
+    q_in,
     kv_ref,
     group_ref,
     slot_ref,
     length_ref,
-    out_hbm,
-    q_in,
     q_send,
     q_recv,
     kv_send,
@@ -80,6 +84,19 @@
         cols = pl.ds(j * WIDE, WIDE)
         return pltpu.make_async_copy(q_hbm.at[0, :, cols], q_in.at[:, cols], in_sem.at[j])
 
+    small = [
+        pltpu.make_async_copy(source, target, in_sem.at[HK + n])
+        for n, (source, target) in enumerate(
+            [
+                (group_hbm, group_ref),
+                (slot_hbm, slot_ref),
+                (kv_hbm, kv_ref),
+                (length_hbm, length_ref),
+            ]
+        )
+    ]
+    for copy in small:
+        copy.start()
     for j in range(HK):
         load(j).start()
 
@@ -101,6 +118,8 @@
     def _():
         greet(me, seq - NX)
 
+    for copy in small:
+        copy.wait()
     targets = group_ref[...]
     lane = lax.broadcasted_iota(jnp.int32, (TOK, TOK), 1)
     sub = lax.broadcasted_iota(jnp.int32, (TOK, TOK), 0)
@@ -266,6 +285,8 @@
         cols = pl.ds(pl.multiple_of(j * WIDE, WIDE), WIDE)
         return pltpu.make_async_copy(out_buf.at[:, cols], out_hbm.at[0, :, cols], out_sem.at[j])
 
+    ones = jnp.ones((SPAN, HD), jnp.bfloat16)
+
     @pl.loop(0, HK)
     def _(j):
         @pl.loop(1, GROUPS)
@@ -278,17 +299,15 @@
         key_cols = pl.ds(pl.multiple_of(j * HD, HD), HD)
         value_cols = pl.ds(pl.multiple_of((HK + j) * HD, HD), HD)
 
-        @pl.loop(0, HQ // HK)
-        def _(h):
+        for h in range(HQ // HK):
             keys = window[pl.ds(x, BACK + 1), :, key_cols].reshape(SPAN, HD)
             values = window[pl.ds(x, BACK + 1), :, value_cols].reshape(SPAN, HD)
             scores = contract(placed[h], keys, ((1,), (1,))) + mask[...]
             top = jnp.max(scores, axis=1, keepdims=True)
-            raised = jnp.exp2((scores - top) * FACTOR)
-            total = jnp.sum(raised, axis=1, keepdims=True)
-            summed = contract(raised.astype(jnp.bfloat16), values, ((1,), (0,)))
+            weights = jnp.exp2((scores - top) * FACTOR).astype(jnp.bfloat16)
+            summed = contract(weights, jnp.concatenate([values, ones], axis=1), ((1,), (0,)))
             cols = pl.ds(pl.multiple_of((j * (HQ // HK) + h) * HD, HD), HD)
-            out_buf[:, cols] = (summed / total).astype(jnp.bfloat16)
+            out_buf[:, cols] = (summed[:, :HD] / summed[:, HD:]).astype(jnp.bfloat16)
 
         store(j).start()
 
@@ -327,15 +346,19 @@
         kernel,
         out_shape=jax.ShapeDtypeStruct((1, TOK, HQ * HD), bf16),
         in_specs=[
-            pl.BlockSpec(memory_space=pl.ANY),
-            pl.BlockSpec(memory_space=pltpu.VMEM),
-            pl.BlockSpec(memory_space=pltpu.VMEM),
-            pl.BlockSpec(memory_space=pltpu.VMEM),
-            pl.BlockSpec(memory_space=pltpu.SMEM),
+            pl.BlockSpec(memory_space=pltpu.HBM),
+            pl.BlockSpec(memory_space=pltpu.HBM),
+            pl.BlockSpec(memory_space=pltpu.HBM),
+            pl.BlockSpec(memory_space=pltpu.HBM),
+            pl.BlockSpec(memory_space=pltpu.HBM),
         ],
         out_specs=pl.BlockSpec(memory_space=pl.ANY),
         scratch_shapes=[
             pltpu.VMEM((TOK, HQ * HD), bf16),
+            pltpu.VMEM((1, TOK, PAIR), bf16),
+            pltpu.VMEM((1, TOK), jnp.int32),
+            pltpu.VMEM((1, TOK), jnp.int32),
+            pltpu.SMEM((1, 2, 3), jnp.int32),
             pltpu.VMEM((HK, GROUPS, CAP, WIDE), bf16),
             pltpu.VMEM((HK, GROUPS, CAP, WIDE), bf16),
             pltpu.VMEM((GROUPS, CAP, PAIR + TOK), bf16),
@@ -344,7 +367,7 @@
             pltpu.VMEM((TOK, SPAN), jnp.float32),
             pltpu.VMEM((HQ // HK, TOK, HD), bf16),
             pltpu.VMEM((TOK, HQ * HD), bf16),
-            dma((HK,)),
+            dma((HK + 4,)),
             dma((HK,)),
             dma((HK, GROUPS)),
             dma((HK, GROUPS)),
@@ -356,7 +379,7 @@
             dma((3, NX)),
         ],
         compiler_params=pltpu.CompilerParams(
-            collective_id=0, has_side_effects=True, vmem_limit_bytes=48 << 20
+            collective_id=0, has_side_effects=True, vmem_limit_bytes=63 << 20
         ),
     )(queries, keys_values, route_group, route_slot, doc_lengths)
 

time: 85.1 us -> 79.4 us (0.933)
  local copies, waits for them, and re-layouts: 5.13 us -> 2.29 us
  Pallas kernels: 79.3 us -> 76.9 us
    unnamed x11 -> x1, local copies, waits for them, and re-layouts: 5.13 us -> 2.29 us
    pallas_call x1, Pallas kernels: 79.3 us -> 76.9 us  [local(): pl.pallas_call(kernel, out_shape=jax.ShapeDtypeStruct((1, TOK, HQ * HD),...]
where the time goes in v1:
time: 79.4 us; the launch traced here: 79.2 us
  Pallas kernels  76.9 us (97%)
  local copies, waits for them, and re-layouts  2.29 us (3%)
    pallas_call x1, Pallas kernels, local(): pl.pallas_call(kernel, out_shape=jax.ShapeDtypeStruct((1, TOK, HQ * HD),...  76.9 us
    unnamed x1, local copies, waits for them, and re-layouts  2.29 us

profile of v1, /device:TPU:1, one launch (start us, length us, event | category | flops | bytes accessed | tf_op | source)
XLA Modules:
  0.0 79.2 jit_solution(4827252762279734334)
XLA Ops:
  0.0 76.9 %shard_map.55 = bf16[1,128,4096]{2,1,0:T(8,128)(2,1)} custom-call(bf16[1,128,4096]{2,1,0:T(8,128)(2,1)} %q_hbm.1, bf16[1,128,1024]{2,1,0:T(8,128)(2,1)} %kv_hbm.1, s32[1,128]{1,0:T(1,128)} %group_hbm.1, s32[1,128]{1,0:T(1,128)} %slot_hbm.1, s32[1,2,3]{2,1,0:T(2,128)} %length_hbm.1), custom_call_target="tpu_custom_call" | custom-call | tf_op jit(solution)/shard_map/pallas_call | solution.py:345
  76.9 2.3 %copy.7 = bf16[1,128,4096]{2,1,0:T(8,128)(2,1)} copy(bf16[1,128,4096]{2,1,0:T(8,128)(2,1)} %shard_map.55) | data formatting | bytes 2097152

commit v2 on v1

--- a/solution.py
+++ b/solution.py
@@ -41,7 +41,7 @@
     return lax.dot_general(a, b, (dims, ((), ())), preferred_element_type=jnp.float32)
 
 
-def kernel(
+def padded_kernel(
     q_hbm,
     kv_hbm,
     group_hbm,
@@ -339,11 +339,11 @@
         each_x(0, sent_x, True)
 
 
-def local(queries, keys_values, route_group, route_slot, doc_lengths):
+def padded(queries, keys_values, route_group, route_slot, doc_lengths):
     bf16 = jnp.bfloat16
     dma = pltpu.SemaphoreType.DMA
     return pl.pallas_call(
-        kernel,
+        padded_kernel,
         out_shape=jax.ShapeDtypeStruct((1, TOK, HQ * HD), bf16),
         in_specs=[
             pl.BlockSpec(memory_space=pltpu.HBM),
@@ -379,9 +379,554 @@
             dma((3, NX)),
         ],
         compiler_params=pltpu.CompilerParams(
-            collective_id=0, has_side_effects=True, vmem_limit_bytes=63 << 20
+            collective_id=0, has_side_effects=True, vmem_limit_bytes=64 << 20
         ),
     )(queries, keys_values, route_group, route_slot, doc_lengths)
+
+
+LOW = 8
+OVER = 8
+HALF_WIDE = WIDE // 2
+PIECE = PAIR // 2
+NY = GROUPS // 2
+NZ = 2 * HALF_ROWS
+
+
+def both_halves(one):
+    none = jnp.zeros_like(one)
+    left = jnp.concatenate([one, none], axis=1)
+    right = jnp.concatenate([none, one], axis=1)
+    lanes = one.shape[2]
+    return jnp.concatenate([left.reshape(-1, lanes), right.reshape(-1, lanes)], axis=1)
+
+
+def compact_kernel(
+    q_hbm,
+    kv_hbm,
+    group_hbm,
+    slot_hbm,
+    length_hbm,
+    out_hbm,
+    flag_ref,
+    q_in,
+    kv_ref,
+    group_ref,
+    slot_ref,
+    length_ref,
+    q_send,
+    q_recv,
+    kva_send,
+    kva_recv,
+    kvb_send,
+    kvb_recv,
+    over,
+    window,
+    mask,
+    placed,
+    out_buf,
+    flag_x,
+    flag_z,
+    in_sem,
+    out_sem,
+    q_ss,
+    q_rs,
+    kv_ss,
+    kv_rs,
+    ring_ss,
+    ring_rs,
+    sib_ss,
+    sib_rs,
+    z_ss,
+    z_rs,
+    x_ss,
+    x_rs,
+    fx_ss,
+    fx_rs,
+    fz_ss,
+    fz_rs,
+):
+    bf16 = jnp.bfloat16
+    f32 = jnp.float32
+    me = lax.axis_index("grp")
+    seq = lax.axis_index("seq")
+    z = seq // NX
+    x = seq % NX
+    zz = z % HALF_ROWS
+    y = me // 2
+    core = me % 2
+    has_next = zz < HALF_ROWS - 1
+    has_last = zz > 0
+
+    small = [
+        pltpu.make_async_copy(source, target, in_sem.at[2 * HK + n])
+        for n, (source, target) in enumerate(
+            [
+                (group_hbm, group_ref),
+                (slot_hbm, slot_ref),
+                (kv_hbm, kv_ref),
+                (length_hbm, length_ref),
+            ]
+        )
+    ]
+    loads = [
+        pltpu.make_async_copy(
+            q_hbm.at[0, :, pl.ds(n * HALF_WIDE, HALF_WIDE)], q_in.at[n], in_sem.at[n]
+        )
+        for n in range(2 * HK)
+    ]
+    for copy in small + loads:
+        copy.start()
+
+    barrier = pltpu.get_barrier_semaphore()
+
+    def greet(group, place):
+        pl.semaphore_signal(barrier, inc=1, device_id=(group, place), device_id_type=MESH)
+
+    for d in range(1, GROUPS):
+        greet((me + d) % GROUPS, seq)
+    for d in range(1, NX):
+        greet(me, z * NX + (x + d) % NX)
+    for d in range(1, NZ):
+        greet(me, (z + d) % NZ * NX + x)
+
+    for copy in small:
+        copy.wait()
+    targets = group_ref[...]
+    lane = lax.broadcasted_iota(jnp.int32, (TOK, TOK), 1)
+    sub = lax.broadcasted_iota(jnp.int32, (TOK, TOK), 0)
+    hits = lax.broadcasted_iota(jnp.int32, (GROUPS, TOK), 0) == targets
+    before = (sub < lane).astype(f32).astype(bf16)
+    all_ones = jnp.ones((TOK, TOK), bf16)
+    ranks = contract(hits.astype(f32).astype(bf16), before, ((1,), (0,)))
+    ranks = jnp.where(hits, ranks, -1.0)
+    level = lax.broadcasted_iota(jnp.int32, (GROUPS, CAP, TOK), 1).astype(f32)
+    pick_three = (ranks[:, None, :] == level).astype(f32)
+    pick_f = pick_three.reshape(SLOTS, TOK)
+    pick = pick_f.astype(bf16)
+    places = (slot_ref[...] + 1).astype(f32)
+    beyond = jnp.sum((ranks >= LOW).astype(f32), axis=0, keepdims=True)
+    order = contract(jnp.broadcast_to(beyond, (OVER, TOK)).astype(bf16), before, ((1,), (0,)))
+    row = lax.broadcasted_iota(jnp.int32, (OVER, TOK), 0).astype(f32)
+    extra = jnp.where((order == row) & (beyond > 0.0), 1.0, 0.0)
+    crowded = jnp.sum(beyond, axis=1, keepdims=True) > OVER
+    marks = contract((pick_f * places).astype(bf16), all_ones, ((1,), (0,)))
+    marks = jnp.where(crowded, -1.0, marks)
+    kva_send[:, :, PIECE:] = marks.astype(bf16).reshape(GROUPS, CAP, TOK)
+
+    sends = [kva_send, kvb_send]
+    recvs = [kva_recv, kvb_recv]
+
+    def pack_pairs(n):
+        for part in range(2):
+            cols = kv_ref[0, :, part * PIECE + n * PIECE // 2 : part * PIECE + (n + 1) * PIECE // 2]
+            sends[n][:, :, part * PIECE // 2 : (part + 1) * PIECE // 2] = (
+                contract(pick, cols, ((1,), (0,))).astype(bf16).reshape(GROUPS, CAP, PIECE // 2)
+            )
+
+    def kv_copy(n, d):
+        target = (me + d) % GROUPS
+        return remote(
+            sends[n].at[target], recvs[n].at[me], kv_ss.at[n, d], kv_rs.at[n, d], (target, seq)
+        )
+
+    def start_pairs(n):
+        @pl.loop(1, GROUPS)
+        def _(d):
+            kv_copy(n, d).start()
+
+        recvs[n][me] = sends[n][me]
+
+    high = both_halves(extra[None]).astype(bf16)
+    for j in range(HK):
+        loads[2 * j].wait()
+        loads[2 * j + 1].wait()
+        halves = q_in[2 * j : 2 * j + 2].reshape(2 * TOK, HALF_WIDE)
+        over[me, :, j * HALF_WIDE : (j + 1) * HALF_WIDE] = contract(
+            high, halves, ((1,), (0,))
+        ).astype(bf16)
+    tags = jnp.concatenate([extra * places, extra * (targets + 1).astype(f32)], axis=0)
+    over[me, :, HK * HALF_WIDE :] = contract(tags.astype(bf16), all_ones, ((1,), (0,))).astype(bf16)
+    pack_pairs(0)
+
+    turn = 1 - 2 * core
+
+    def on_ring(at):
+        return (at + 2 * NY) % NY * 2 + core
+
+    def on_sibling(at):
+        return (at + 2 * NY) % NY * 2 + 1 - core
+
+    def ring(step, way):
+        sign = turn if way == 0 else -turn
+        block = on_ring(y - sign * (step - 1))
+        return remote(
+            over.at[block],
+            over.at[block],
+            ring_ss.at[way, step],
+            ring_rs.at[way, step],
+            (on_ring(y + sign), seq),
+        )
+
+    def ring_came(step, way):
+        sign = turn if way == 0 else -turn
+        block = on_ring(y - sign * step)
+        remote(
+            over.at[block],
+            over.at[block],
+            ring_ss.at[way, step],
+            ring_rs.at[way, step],
+            (on_ring(y + sign), seq),
+        ).wait_recv()
+
+    def sibling(n):
+        block = on_ring(y - turn * n if n <= NY // 2 else y + turn * (n - NY // 2))
+        return remote(
+            over.at[block], over.at[block], sib_ss.at[n], sib_rs.at[n], (on_sibling(y), seq)
+        )
+
+    def sibling_came(n):
+        block = on_sibling(y + turn * n if n <= NY // 2 else y - turn * (n - NY // 2))
+        remote(
+            over.at[block], over.at[block], sib_ss.at[n], sib_rs.at[n], (on_sibling(y), seq)
+        ).wait_recv()
+
+    def ring_turn(step):
+        ring_came(step, 0)
+        if step < NY // 2:
+            ring(step + 1, 0).start()
+            ring_came(step, 1)
+            if step + 1 < NY // 2:
+                ring(step + 1, 1).start()
+            sibling(NY // 2 + step).start()
+        sibling(step).start()
+
+    pl.semaphore_wait(barrier, GROUPS - 1 + NX - 1 + NZ - 1)
+    ring(1, 0).start()
+    ring(1, 1).start()
+    start_pairs(0)
+    sibling(0).start()
+    pack_pairs(1)
+    start_pairs(1)
+
+    low = both_halves(pick_three[:, :LOW]).astype(bf16)
+    for j in range(HK):
+        halves = q_in[2 * j : 2 * j + 2].reshape(2 * TOK, HALF_WIDE)
+        q_send[j] = (
+            contract(low, halves, ((1,), (0,))).astype(bf16).reshape(GROUPS, CAP, HALF_WIDE)
+        )
+
+    def q_copy(j, d):
+        target = (me + d) % GROUPS
+        return remote(
+            q_send.at[j, target], q_recv.at[j, me], q_ss.at[j, d], q_rs.at[j, d], (target, seq)
+        )
+
+    def start_queries(j):
+        @pl.loop(1, GROUPS)
+        def _(d):
+            q_copy(j, d).start()
+
+        q_recv[j, me] = q_send[j, me]
+
+    start_queries(0)
+
+    query = seq * TOK + lax.broadcasted_iota(jnp.int32, (TOK, SPAN), 0)
+    key = (seq - BACK) * TOK + lax.broadcasted_iota(jnp.int32, (TOK, SPAN), 1)
+    begin = jnp.zeros((TOK, SPAN), jnp.int32)
+    bound = jnp.int32(0)
+    for half in range(2):
+        for n in range(3):
+            bound = bound + length_ref[0, half, n]
+            begin = jnp.where(query >= bound, bound, begin)
+    mask[...] = jnp.where((key >= begin) & (key <= query), 0.0, NEGATIVE)
+
+    @pl.when(zz == 0)
+    def _():
+        window[:, pl.ds(0, 2 * NX)] = jnp.zeros((2, 2 * NX, TOK, PIECE), bf16)
+
+    @pl.when(zz == 1)
+    def _():
+        window[:, pl.ds(0, NX)] = jnp.zeros((2, NX, TOK, PIECE), bf16)
+
+    def z_copy(n, plane):
+        return remote(
+            window.at[n, plane * NX + x],
+            window.at[n, (plane - 1) * NX + x],
+            z_ss.at[n, plane],
+            z_rs.at[n, plane],
+            (me, (seq + NX) % (NX * NZ)),
+        )
+
+    def x_copy(n, plane, d, came=False):
+        at = plane * NX + ((x + NX - d) % NX if came else x)
+        return remote(
+            window.at[n, at],
+            window.at[n, at],
+            x_ss.at[n, plane, d],
+            x_rs.at[n, plane, d],
+            (me, z * NX + (x + d) % NX),
+        )
+
+    def start_x(n, plane, d):
+        x_copy(n, plane, d).start()
+
+    def sent_x(n, plane, d):
+        x_copy(n, plane, d).wait_send()
+
+    def came_x(n, plane, d):
+        x_copy(n, plane, d, True).wait_recv()
+
+    def each_x(n, plane, act):
+        for d in range(1, NX):
+            wraps = x - d < 0 if act is came_x else x + d >= NX
+            if plane == 1:
+                act(n, plane, d)
+            else:
+                pl.when(wraps if plane == 0 else jnp.logical_not(wraps))(
+                    functools.partial(act, n, plane, d)
+                )
+
+    def place_pairs(n):
+        window[n, 2 * NX + x] = contract(
+            put, recvs[n][:, :, :PIECE].reshape(SLOTS, PIECE), ((1,), (0,))
+        ).astype(bf16)
+
+        @pl.when(has_next)
+        def _():
+            z_copy(n, 2).start()
+
+        each_x(n, 2, start_x)
+
+    def one_back(n):
+        @pl.when(has_last)
+        def _():
+            z_copy(n, 2).wait_recv()
+
+            @pl.when(has_next)
+            def _():
+                z_copy(n, 1).start()
+
+            each_x(n, 1, start_x)
+
+    def two_back(n):
+        @pl.when(zz >= 2)
+        def _():
+            z_copy(n, 1).wait_recv()
+            each_x(n, 0, start_x)
+
+    def flag_x_copy(d, came=False):
+        at = (x + NX - d) % NX if came else x
+        return remote(
+            flag_x.at[at],
+            flag_x.at[at],
+            fx_ss.at[d],
+            fx_rs.at[d],
+            (me, z * NX + (x + d) % NX),
+        )
+
+    def flag_z_copy(d, came=False):
+        at = (z + NZ - d) % NZ if came else z
+        return remote(
+            flag_z.at[at],
+            flag_z.at[at],
+            fz_ss.at[d],
+            fz_rs.at[d],
+            (me, (z + d) % NZ * NX + x),
+        )
+
+    def pairs_came(n):
+        @pl.loop(1, GROUPS)
+        def _(d):
+            kv_copy(n, d).wait_recv()
+
+    ring_turn(1)
+    pairs_came(0)
+    marks_in = kva_recv[:, :, PIECE:].astype(f32)
+    column = lax.broadcasted_iota(jnp.int32, (GROUPS, CAP, TOK), 2).astype(f32) + 1.0
+    match = (marks_in == column).astype(f32)
+    put = match.reshape(SLOTS, TOK).T.astype(bf16)
+    place_pairs(0)
+    worst = jnp.max((marks_in < 0.0).astype(f32).reshape(SLOTS, TOK), axis=0, keepdims=True)
+    flag_x[x] = jnp.broadcast_to(worst, (CAP, TOK)).astype(bf16)
+    for d in range(1, NX):
+        flag_x_copy(d).start()
+    put_low = both_halves(match[:, :LOW]).T.astype(bf16)
+
+    ring_turn(2)
+    pairs_came(1)
+    place_pairs(1)
+    start_queries(1)
+    for d in range(1, NX):
+        flag_x_copy(d, True).wait_recv()
+    flag_z[z] = jnp.max(flag_x[...].astype(f32), axis=0).astype(bf16)
+    for d in range(1, NZ):
+        flag_z_copy(d).start()
+    ring_turn(3)
+    one_back(0)
+    one_back(1)
+    start_queries(2)
+    ring_turn(4)
+    two_back(0)
+    start_queries(3)
+    two_back(1)
+    for d in range(1, NZ):
+        flag_z_copy(d, True).wait_recv()
+    flag_ref[0, 0] = jnp.max(flag_z[...].astype(f32)).astype(jnp.int32)
+    for n in range(NY):
+        sibling_came(n)
+
+    tags_in = over[:, :, HK * HALF_WIDE :].astype(f32)
+    mine = (me + 1).astype(f32)
+    match_over = ((tags_in[:, :OVER] == column[:, :OVER]) & (tags_in[:, OVER:] == mine)).astype(f32)
+    put_over = both_halves(match_over).T.astype(bf16)
+
+    def store(j):
+        cols = pl.ds(pl.multiple_of(j * WIDE, WIDE), WIDE)
+        return pltpu.make_async_copy(out_buf.at[:, cols], out_hbm.at[0, :, cols], out_sem.at[j])
+
+    ones = jnp.ones((SPAN, HD), bf16)
+
+    def window_came(n):
+        each_x(n, 2, came_x)
+
+        @pl.when(has_last)
+        def _():
+            each_x(n, 1, came_x)
+
+        @pl.when(zz >= 2)
+        def _():
+            each_x(n, 0, came_x)
+
+    @pl.loop(0, HK)
+    def _(j):
+        pl.when(j == 0)(functools.partial(window_came, 0))
+        pl.when(j == HK // 2)(functools.partial(window_came, 1))
+
+        @pl.loop(1, GROUPS)
+        def _(d):
+            q_copy(j, d).wait_recv()
+
+        cols = pl.ds(pl.multiple_of(j * HALF_WIDE, HALF_WIDE), HALF_WIDE)
+        rows = contract(put_low, q_recv[j].reshape(SLOTS, HALF_WIDE), ((1,), (0,)))
+        rows = rows + contract(put_over, over[:, :, cols].reshape(SLOTS, HALF_WIDE), ((1,), (0,)))
+        rows = rows.astype(bf16)
+        for h in range(HQ // HK):
+            half, at = h // (HQ // HK // 2), h % (HQ // HK // 2)
+            placed[h] = rows[half * TOK : (half + 1) * TOK, at * HD : (at + 1) * HD]
+        key_cols = pl.ds(pl.multiple_of(j % 2 * HD, HD), HD)
+        value_cols = pl.ds(pl.multiple_of(PIECE // 2 + j % 2 * HD, HD), HD)
+        for h in range(HQ // HK):
+            keys = window[j // 2, pl.ds(x, BACK + 1), :, key_cols].reshape(SPAN, HD)
+            values = window[j // 2, pl.ds(x, BACK + 1), :, value_cols].reshape(SPAN, HD)
+            scores = contract(placed[h], keys, ((1,), (1,))) + mask[...]
+            top = jnp.max(scores, axis=1, keepdims=True)
+            weights = jnp.exp2((scores - top) * FACTOR).astype(bf16)
+            summed = contract(weights, jnp.concatenate([values, ones], axis=1), ((1,), (0,)))
+            head_cols = pl.ds(pl.multiple_of((j * (HQ // HK) + h) * HD, HD), HD)
+            out_buf[:, head_cols] = (summed[:, :HD] / summed[:, HD:]).astype(bf16)
+
+        store(j).start()
+
+    for j in range(HK):
+        store(j).wait()
+
+    @pl.loop(1, GROUPS)
+    def _(d):
+        for n in range(2):
+            kv_copy(n, d).wait_send()
+        for j in range(HK):
+            q_copy(j, d).wait_send()
+
+    for n in range(2):
+        each_x(n, 2, sent_x)
+
+        @pl.when(has_next)
+        def _(n=n):
+            z_copy(n, 2).wait_send()
+
+        @pl.when(has_last)
+        def _(n=n):
+            each_x(n, 1, sent_x)
+
+            @pl.when(has_next)
+            def _():
+                z_copy(n, 1).wait_send()
+
+        @pl.when(zz >= 2)
+        def _(n=n):
+            each_x(n, 0, sent_x)
+
+    for step in range(1, NY // 2 + 1):
+        ring(step, 0).wait_send()
+        if step < NY // 2:
+            ring(step, 1).wait_send()
+    for n in range(NY):
+        sibling(n).wait_send()
+    for d in range(1, NX):
+        flag_x_copy(d).wait_send()
+    for d in range(1, NZ):
+        flag_z_copy(d).wait_send()
+
+
+def compact(*operands):
+    bf16 = jnp.bfloat16
+    dma = pltpu.SemaphoreType.DMA
+    vmem = pltpu.VMEM
+    return pl.pallas_call(
+        compact_kernel,
+        out_shape=(
+            jax.ShapeDtypeStruct((1, TOK, HQ * HD), bf16),
+            jax.ShapeDtypeStruct((1, 1), jnp.int32),
+        ),
+        in_specs=[pl.BlockSpec(memory_space=pltpu.HBM)] * 5,
+        out_specs=(pl.BlockSpec(memory_space=pl.ANY), pl.BlockSpec(memory_space=pltpu.SMEM)),
+        scratch_shapes=[
+            vmem((2 * HK, TOK, HALF_WIDE), bf16),
+            vmem((1, TOK, PAIR), bf16),
+            vmem((1, TOK), jnp.int32),
+            vmem((1, TOK), jnp.int32),
+            pltpu.SMEM((1, 2, 3), jnp.int32),
+            vmem((HK, GROUPS, CAP, HALF_WIDE), bf16),
+            vmem((HK, GROUPS, CAP, HALF_WIDE), bf16),
+            vmem((GROUPS, CAP, PIECE + TOK), bf16),
+            vmem((GROUPS, CAP, PIECE + TOK), bf16),
+            vmem((GROUPS, CAP, PIECE), bf16),
+            vmem((GROUPS, CAP, PIECE), bf16),
+            vmem((GROUPS, CAP, HK * HALF_WIDE + TOK), bf16),
+            vmem((2, 3 * NX, TOK, PIECE), bf16),
+            vmem((TOK, SPAN), jnp.float32),
+            vmem((HQ // HK, TOK, HD), bf16),
+            vmem((TOK, HQ * HD), bf16),
+            vmem((NX, CAP, TOK), bf16),
+            vmem((NZ, CAP, TOK), bf16),
+            dma((2 * HK + 4,)),
+            dma((HK,)),
+            dma((HK, GROUPS)),
+            dma((HK, GROUPS)),
+            dma((2, GROUPS)),
+            dma((2, GROUPS)),
+            dma((2, NY // 2 + 1)),
+            dma((2, NY // 2 + 1)),
+            dma((NY,)),
+            dma((NY,)),
+            dma((2, 3)),
+            dma((2, 3)),
+            dma((2, 3, NX)),
+            dma((2, 3, NX)),
+            dma((NX,)),
+            dma((NX,)),
+            dma((NZ,)),
+            dma((NZ,)),
+        ],
+        compiler_params=pltpu.CompilerParams(
+            collective_id=1, has_side_effects=True, vmem_limit_bytes=64 << 20
+        ),
+    )(*operands)
+
+
+def local(*operands):
+    result, crowded = compact(*operands)
+    return lax.switch(crowded[0, 0], [lambda: result, lambda: padded(*operands)])
 
 
 def solution(mesh):

time: 79.4 us -> 78.2 us (0.985)
  the two profiles are of different devices: /device:TPU:1 before, /device:TPU:160 now
where the time goes in v2:
time: 78.2 us; the launch traced here: 78 us
  Pallas kernels  75 us (96%)
  local copies, waits for them, and re-layouts  2.29 us (3%)
    pallas_call x1, Pallas kernels, compact(): pl.pallas_call(compact_kernel, out_shape=(jax.ShapeDtypeStruct((1, TOK, H...  75 us
    unnamed x1, local copies, waits for them, and re-layouts  2.29 us

profile of v2, /device:TPU:160, one launch (start us, length us, event | category | flops | bytes accessed | tf_op | source)
XLA Modules:
  0.0 78.0 jit_solution(7137170986765605499)
XLA Ops:
  0.0 75.0 %shard_map.57 = (bf16[1,128,4096]{2,1,0:T(8,128)(2,1)}, s32[1,1]{1,0:T(1,128)}) custom-call(bf16[1,128,4096]{2,1,0:T(8,128)(2,1)} %q_hbm.1, bf16[1,128,1024]{2,1,0:T(8,128)(2,1)} %kv_hbm.1, s32[1,128]{1,0:T(1,128)} %group_hbm.1, s32[1,128]{1,0:T(1,128)} %slot_hbm.1, s32[1,2,3]{2,1,0:T(2,128)} %length_hbm.1), custom_call_target="tpu_custom_call" | custom-call | tf_op jit(solution)/shard_map/pallas_call | solution.py:875
  75.7 2.3 %copy.11 = bf16[1,128,4096]{2,1,0:T(8,128)(2,1)} copy(bf16[1,128,4096]{2,1,0:T(8,128)(2,1)} %get-tuple-element.28) | data formatting | bytes 2097152
  (1 shorter events, 0.0 us)

commit v3 on v2

--- a/solution.py
+++ b/solution.py
@@ -523,17 +523,26 @@
                 contract(pick, cols, ((1,), (0,))).astype(bf16).reshape(GROUPS, CAP, PIECE // 2)
             )
 
+    def partner(d):
+        return (y + d // 2) % NY * 2 + (core + d % 2) % 2
+
+    def far_first(act):
+        @pl.loop(0, NY - 1)
+        def _(i):
+            away = NY // 2 + i // 2 * (1 - i % 2) - (i + 1) // 2 * (i % 2)
+            act(2 * away)
+            act(2 * away + 1)
+
+        act(1)
+
     def kv_copy(n, d):
-        target = (me + d) % GROUPS
+        target = partner(d)
         return remote(
             sends[n].at[target], recvs[n].at[me], kv_ss.at[n, d], kv_rs.at[n, d], (target, seq)
         )
 
     def start_pairs(n):
-        @pl.loop(1, GROUPS)
-        def _(d):
-            kv_copy(n, d).start()
-
+        far_first(lambda d: kv_copy(n, d).start())
         recvs[n][me] = sends[n][me]
 
     high = both_halves(extra[None]).astype(bf16)
@@ -616,19 +625,14 @@
         )
 
     def q_copy(j, d):
-        target = (me + d) % GROUPS
+        target = partner(d)
         return remote(
             q_send.at[j, target], q_recv.at[j, me], q_ss.at[j, d], q_rs.at[j, d], (target, seq)
         )
 
     def start_queries(j):
-        @pl.loop(1, GROUPS)
-        def _(d):
-            q_copy(j, d).start()
-
+        far_first(lambda d: q_copy(j, d).start())
         q_recv[j, me] = q_send[j, me]
-
-    start_queries(0)
 
     query = seq * TOK + lax.broadcasted_iota(jnp.int32, (TOK, SPAN), 0)
     key = (seq - BACK) * TOK + lax.broadcasted_iota(jnp.int32, (TOK, SPAN), 1)
@@ -676,8 +680,8 @@
     def came_x(n, plane, d):
         x_copy(n, plane, d, True).wait_recv()
 
-    def each_x(n, plane, act):
-        for d in range(1, NX):
+    def each_x(n, plane, act, steps):
+        for d in steps:
             wraps = x - d < 0 if act is came_x else x + d >= NX
             if plane == 1:
                 act(n, plane, d)
@@ -686,6 +690,43 @@
                     functools.partial(act, n, plane, d)
                 )
 
+    beside = (1, NX - 1)
+    inner = (x == 1) | (x == 2)
+
+    def pass_on(n, plane, way, slot):
+        at = plane * NX + (x + NX - way) % NX
+        return remote(
+            window.at[n, at],
+            window.at[n, at],
+            x_ss.at[n, plane, slot],
+            x_rs.at[n, plane, 2],
+            (me, z * NX + (x + NX + way) % NX),
+        )
+
+    def each_pass(n, plane, act):
+        if plane == 1:
+
+            @pl.when(jnp.logical_not(inner))
+            def _():
+                act(pass_on(n, plane, 1, 0))
+                act(pass_on(n, plane, -1, 2))
+
+        else:
+
+            @pl.when(inner)
+            def _():
+                act(pass_on(n, plane, 1 if plane == 2 else -1, 2))
+
+    def forward(n, plane):
+        def go():
+            each_x(n, plane, came_x, beside)
+            each_pass(n, plane, lambda copy: copy.start())
+
+        if plane == 2:
+            go()
+        else:
+            pl.when(has_last if plane == 1 else zz >= 2)(go)
+
     def place_pairs(n):
         window[n, 2 * NX + x] = contract(
             put, recvs[n][:, :, :PIECE].reshape(SLOTS, PIECE), ((1,), (0,))
@@ -695,7 +736,7 @@
         def _():
             z_copy(n, 2).start()
 
-        each_x(n, 2, start_x)
+        each_x(n, 2, start_x, beside)
 
     def one_back(n):
         @pl.when(has_last)
@@ -706,13 +747,13 @@
             def _():
                 z_copy(n, 1).start()
 
-            each_x(n, 1, start_x)
+            each_x(n, 1, start_x, beside)
 
     def two_back(n):
         @pl.when(zz >= 2)
         def _():
             z_copy(n, 1).wait_recv()
-            each_x(n, 0, start_x)
+            each_x(n, 0, start_x, beside)
 
     def flag_x_copy(d, came=False):
         at = (x + NX - d) % NX if came else x
@@ -740,6 +781,7 @@
             kv_copy(n, d).wait_recv()
 
     ring_turn(1)
+    start_queries(0)
     pairs_came(0)
     marks_in = kva_recv[:, :, PIECE:].astype(f32)
     column = lax.broadcasted_iota(jnp.int32, (GROUPS, CAP, TOK), 2).astype(f32) + 1.0
@@ -753,22 +795,28 @@
     put_low = both_halves(match[:, :LOW]).T.astype(bf16)
 
     ring_turn(2)
+    start_queries(1)
     pairs_came(1)
     place_pairs(1)
-    start_queries(1)
+    forward(0, 2)
+    one_back(0)
     for d in range(1, NX):
         flag_x_copy(d, True).wait_recv()
     flag_z[z] = jnp.max(flag_x[...].astype(f32), axis=0).astype(bf16)
     for d in range(1, NZ):
         flag_z_copy(d).start()
     ring_turn(3)
-    one_back(0)
+    start_queries(2)
     one_back(1)
-    start_queries(2)
+    two_back(0)
+    forward(1, 2)
+    forward(0, 1)
+    two_back(1)
     ring_turn(4)
-    two_back(0)
     start_queries(3)
-    two_back(1)
+    forward(0, 0)
+    forward(1, 1)
+    forward(1, 0)
     for d in range(1, NZ):
         flag_z_copy(d, True).wait_recv()
     flag_ref[0, 0] = jnp.max(flag_z[...].astype(f32)).astype(jnp.int32)
@@ -787,15 +835,15 @@
     ones = jnp.ones((SPAN, HD), bf16)
 
     def window_came(n):
-        each_x(n, 2, came_x)
+        each_x(n, 2, came_x, (2,))
 
         @pl.when(has_last)
         def _():
-            each_x(n, 1, came_x)
+            each_x(n, 1, came_x, (2,))
 
         @pl.when(zz >= 2)
         def _():
-            each_x(n, 0, came_x)
+            each_x(n, 0, came_x, (2,))
 
     @pl.loop(0, HK)
     def _(j):
@@ -838,7 +886,8 @@
             q_copy(j, d).wait_send()
 
     for n in range(2):
-        each_x(n, 2, sent_x)
+        each_x(n, 2, sent_x, beside)
+        each_pass(n, 2, lambda copy: copy.wait_send())
 
         @pl.when(has_next)
         def _(n=n):
@@ -846,7 +895,8 @@
 
         @pl.when(has_last)
         def _(n=n):
-            each_x(n, 1, sent_x)
+            each_x(n, 1, sent_x, beside)
+            each_pass(n, 1, lambda copy: copy.wait_send())
 
             @pl.when(has_next)
             def _():
@@ -854,7 +904,8 @@
 
         @pl.when(zz >= 2)
         def _(n=n):
-            each_x(n, 0, sent_x)
+            each_x(n, 0, sent_x, beside)
+            each_pass(n, 0, lambda copy: copy.wait_send())
 
     for step in range(1, NY // 2 + 1):
         ring(step, 0).wait_send()

time: 78.2 us -> 68.8 us (0.88)
  the two profiles are of different devices: /device:TPU:160 before, /device:TPU:128 now
where the time goes in v3:
time: 68.8 us; the launch traced here: 68.6 us
  Pallas kernels  65.7 us (95%)
  local copies, waits for them, and re-layouts  2.29 us (3%)
    pallas_call x1, Pallas kernels, compact(): pl.pallas_call(compact_kernel, out_shape=(jax.ShapeDtypeStruct((1, TOK, H...  65.7 us
    unnamed x1, local copies, waits for them, and re-layouts  2.29 us

profile of v3, /device:TPU:128, one launch (start us, length us, event | category | flops | bytes accessed | tf_op | source)
XLA Modules:
  0.0 68.6 jit_solution(16904902007895481503)
XLA Ops:
  0.0 65.7 %shard_map.57 = (bf16[1,128,4096]{2,1,0:T(8,128)(2,1)}, s32[1,1]{1,0:T(1,128)}) custom-call(bf16[1,128,4096]{2,1,0:T(8,128)(2,1)} %q_hbm.1, bf16[1,128,1024]{2,1,0:T(8,128)(2,1)} %kv_hbm.1, s32[1,128]{1,0:T(1,128)} %group_hbm.1, s32[1,128]{1,0:T(1,128)} %slot_hbm.1, s32[1,2,3]{2,1,0:T(2,128)} %length_hbm.1), custom_call_target="tpu_custom_call" | custom-call | tf_op jit(solution)/shard_map/pallas_call | solution.py:926
  66.4 2.3 %copy.11 = bf16[1,128,4096]{2,1,0:T(8,128)(2,1)} copy(bf16[1,128,4096]{2,1,0:T(8,128)(2,1)} %get-tuple-element.28) | data formatting | bytes 2097152
  (1 shorter events, 0.0 us)

commit v4 on v3

--- a/solution.py
+++ b/solution.py
@@ -545,6 +545,8 @@
         far_first(lambda d: kv_copy(n, d).start())
         recvs[n][me] = sends[n][me]
 
+    pack_pairs(0)
+
     high = both_halves(extra[None]).astype(bf16)
     for j in range(HK):
         loads[2 * j].wait()
@@ -555,8 +557,6 @@
         ).astype(bf16)
     tags = jnp.concatenate([extra * places, extra * (targets + 1).astype(f32)], axis=0)
     over[me, :, HK * HALF_WIDE :] = contract(tags.astype(bf16), all_ones, ((1,), (0,))).astype(bf16)
-    pack_pairs(0)
-
     turn = 1 - 2 * core
 
     def on_ring(at):
@@ -615,6 +615,8 @@
     start_pairs(0)
     sibling(0).start()
     pack_pairs(1)
+
+    ring_turn(1)
     start_pairs(1)
 
     low = both_halves(pick_three[:, :LOW]).astype(bf16)
@@ -780,8 +782,6 @@
         def _(d):
             kv_copy(n, d).wait_recv()
 
-    ring_turn(1)
-    start_queries(0)
     pairs_came(0)
     marks_in = kva_recv[:, :, PIECE:].astype(f32)
     column = lax.broadcasted_iota(jnp.int32, (GROUPS, CAP, TOK), 2).astype(f32) + 1.0
@@ -795,28 +795,27 @@
     put_low = both_halves(match[:, :LOW]).T.astype(bf16)
 
     ring_turn(2)
+    start_queries(0)
+    forward(0, 2)
+    one_back(0)
+    ring_turn(3)
     start_queries(1)
     pairs_came(1)
     place_pairs(1)
-    forward(0, 2)
-    one_back(0)
     for d in range(1, NX):
         flag_x_copy(d, True).wait_recv()
     flag_z[z] = jnp.max(flag_x[...].astype(f32), axis=0).astype(bf16)
     for d in range(1, NZ):
         flag_z_copy(d).start()
-    ring_turn(3)
+    forward(0, 1)
+    two_back(0)
+    ring_turn(4)
     start_queries(2)
     one_back(1)
-    two_back(0)
     forward(1, 2)
-    forward(0, 1)
+    forward(0, 0)
+    start_queries(3)
     two_back(1)
-    ring_turn(4)
-    start_queries(3)
-    forward(0, 0)
-    forward(1, 1)
-    forward(1, 0)
     for d in range(1, NZ):
         flag_z_copy(d, True).wait_recv()
     flag_ref[0, 0] = jnp.max(flag_z[...].astype(f32)).astype(jnp.int32)
@@ -847,8 +846,18 @@
 
     @pl.loop(0, HK)
     def _(j):
-        pl.when(j == 0)(functools.partial(window_came, 0))
-        pl.when(j == HK // 2)(functools.partial(window_came, 1))
+        @pl.when(j == 0)
+        def _():
+            window_came(0)
+
+        @pl.when(j == 1)
+        def _():
+            forward(1, 1)
+            forward(1, 0)
+
+        @pl.when(j == 2)
+        def _():
+            window_came(1)
 
         @pl.loop(1, GROUPS)
         def _(d):

time: 68.8 us -> 68.3 us (level)
  no operation moved by 1% of the time
where the time goes in v4:
time: 68.3 us; the launch traced here: 68.1 us
  Pallas kernels  65.2 us (95%)
  local copies, waits for them, and re-layouts  2.29 us (3%)
    pallas_call x1, Pallas kernels, compact(): pl.pallas_call(compact_kernel, out_shape=(jax.ShapeDtypeStruct((1, TOK, H...  65.2 us
    unnamed x1, local copies, waits for them, and re-layouts  2.29 us

profile of v4, /device:TPU:128, one launch (start us, length us, event | category | flops | bytes accessed | tf_op | source)
XLA Modules:
  0.0 68.1 jit_solution(400922175912696447)
XLA Ops:
  0.0 65.2 %shard_map.57 = (bf16[1,128,4096]{2,1,0:T(8,128)(2,1)}, s32[1,1]{1,0:T(1,128)}) custom-call(bf16[1,128,4096]{2,1,0:T(8,128)(2,1)} %q_hbm.1, bf16[1,128,1024]{2,1,0:T(8,128)(2,1)} %kv_hbm.1, s32[1,128]{1,0:T(1,128)} %group_hbm.1, s32[1,128]{1,0:T(1,128)} %slot_hbm.1, s32[1,2,3]{2,1,0:T(2,128)} %length_hbm.1), custom_call_target="tpu_custom_call" | custom-call | tf_op jit(solution)/shard_map/pallas_call | solution.py:935
  65.9 2.3 %copy.11 = bf16[1,128,4096]{2,1,0:T(8,128)(2,1)} copy(bf16[1,128,4096]{2,1,0:T(8,128)(2,1)} %get-tuple-element.28) | data formatting | bytes 2097152
  (1 shorter events, 0.0 us)

commit v5 on v4

--- a/solution.py
+++ b/solution.py
@@ -379,7 +379,7 @@
             dma((3, NX)),
         ],
         compiler_params=pltpu.CompilerParams(
-            collective_id=0, has_side_effects=True, vmem_limit_bytes=64 << 20
+            collective_id=0, has_side_effects=True, vmem_limit_bytes=48 << 20
         ),
     )(queries, keys_values, route_group, route_slot, doc_lengths)
 
@@ -406,7 +406,7 @@
     group_hbm,
     slot_hbm,
     length_hbm,
-    out_hbm,
+    out_ref,
     flag_ref,
     q_in,
     kv_ref,
@@ -423,11 +423,9 @@
     window,
     mask,
     placed,
-    out_buf,
     flag_x,
     flag_z,
     in_sem,
-    out_sem,
     q_ss,
     q_rs,
     kv_ss,
@@ -807,15 +805,15 @@
     flag_z[z] = jnp.max(flag_x[...].astype(f32), axis=0).astype(bf16)
     for d in range(1, NZ):
         flag_z_copy(d).start()
+    two_back(0)
+    start_queries(2)
     forward(0, 1)
-    two_back(0)
-    ring_turn(4)
-    start_queries(2)
     one_back(1)
     forward(1, 2)
+    start_queries(3)
+    ring_turn(4)
+    two_back(1)
     forward(0, 0)
-    start_queries(3)
-    two_back(1)
     for d in range(1, NZ):
         flag_z_copy(d, True).wait_recv()
     flag_ref[0, 0] = jnp.max(flag_z[...].astype(f32)).astype(jnp.int32)
@@ -826,10 +824,6 @@
     mine = (me + 1).astype(f32)
     match_over = ((tags_in[:, :OVER] == column[:, :OVER]) & (tags_in[:, OVER:] == mine)).astype(f32)
     put_over = both_halves(match_over).T.astype(bf16)
-
-    def store(j):
-        cols = pl.ds(pl.multiple_of(j * WIDE, WIDE), WIDE)
-        return pltpu.make_async_copy(out_buf.at[:, cols], out_hbm.at[0, :, cols], out_sem.at[j])
 
     ones = jnp.ones((SPAN, HD), bf16)
 
@@ -880,12 +874,8 @@
             weights = jnp.exp2((scores - top) * FACTOR).astype(bf16)
             summed = contract(weights, jnp.concatenate([values, ones], axis=1), ((1,), (0,)))
             head_cols = pl.ds(pl.multiple_of((j * (HQ // HK) + h) * HD, HD), HD)
-            out_buf[:, head_cols] = (summed[:, :HD] / summed[:, HD:]).astype(bf16)
-
-        store(j).start()
-
-    for j in range(HK):
-        store(j).wait()
+            out_ref[0, :, head_cols] = (summed[:, :HD] / summed[:, HD:]).astype(bf16)
+
 
     @pl.loop(1, GROUPS)
     def _(d):
@@ -935,11 +925,11 @@
     return pl.pallas_call(
         compact_kernel,
         out_shape=(
-            jax.ShapeDtypeStruct((1, TOK, HQ * HD), bf16),
+            pltpu.VMEM((1, TOK, HQ * HD), bf16),
             jax.ShapeDtypeStruct((1, 1), jnp.int32),
         ),
         in_specs=[pl.BlockSpec(memory_space=pltpu.HBM)] * 5,
-        out_specs=(pl.BlockSpec(memory_space=pl.ANY), pl.BlockSpec(memory_space=pltpu.SMEM)),
+        out_specs=(pl.BlockSpec(memory_space=pltpu.VMEM), pl.BlockSpec(memory_space=pltpu.SMEM)),
         scratch_shapes=[
             vmem((2 * HK, TOK, HALF_WIDE), bf16),
             vmem((1, TOK, PAIR), bf16),
@@ -956,11 +946,9 @@
             vmem((2, 3 * NX, TOK, PIECE), bf16),
             vmem((TOK, SPAN), jnp.float32),
             vmem((HQ // HK, TOK, HD), bf16),
-            vmem((TOK, HQ * HD), bf16),
             vmem((NX, CAP, TOK), bf16),
             vmem((NZ, CAP, TOK), bf16),
             dma((2 * HK + 4,)),
-            dma((HK,)),
             dma((HK, GROUPS)),
             dma((HK, GROUPS)),
             dma((2, GROUPS)),
@@ -979,12 +967,13 @@
             dma((NZ,)),
         ],
         compiler_params=pltpu.CompilerParams(
-            collective_id=1, has_side_effects=True, vmem_limit_bytes=64 << 20
+            collective_id=1, has_side_effects=True, vmem_limit_bytes=48 << 20
         ),
     )(*operands)
 
 
 def local(*operands):
+    operands = [pltpu.with_memory_space_constraint(one, pltpu.HBM) for one in operands]
     result, crowded = compact(*operands)
     return lax.switch(crowded[0, 0], [lambda: result, lambda: padded(*operands)])
 

time: 68.3 us -> 64.1 us (0.939)
  the two profiles are of different devices: /device:TPU:128 before, /device:TPU:1 now
where the time goes in v5:
time: 64.1 us; the launch traced here: 63.4 us
  Pallas kernels  61.7 us (96%)
  local copies, waits for them, and re-layouts  0.97 us (2%)
  between operations  0.65 us (1%)
    pallas_call x1, Pallas kernels, compact(): pl.pallas_call(compact_kernel, out_shape=(pltpu.VMEM((1, TOK, HQ * HD), b...  61.7 us

profile of v5, /device:TPU:1, one launch (start us, length us, event | category | flops | bytes accessed | tf_op | source)
XLA Modules:
  0.0 63.4 jit_solution(8717341195140315732)
XLA Ops:
  0.0 61.7 %shard_map.57 = (bf16[1,128,4096]{2,1,0:T(8,128)(2,1)S(1)}, s32[1,1]{1,0:T(1,128)}) custom-call(bf16[1,128,4096]{2,1,0:T(8,128)(2,1)} %q_hbm.1, bf16[1,128,1024]{2,1,0:T(8,128)(2,1)} %kv_hbm.1, s32[1,128]{1,0:T(1,128)} %group_hbm.1, s32[1,128]{1,0:T(1,128)} %slot_hbm.1, s32[1,2,3]{2,1,0:T(2,128)} %length_hbm.1), custom_call_target="tpu_custom_call" | custom-call | tf_op jit(solution)/shard_map/pallas_call | solution.py:925
  62.4 1.0 %copy.11 = bf16[1,128,4096]{2,1,0:T(8,128)(2,1)} copy(bf16[1,128,4096]{2,1,0:T(8,128)(2,1)S(1)} %get-tuple-element.28) | data formatting | bytes 2097152
  (1 shorter events, 0.0 us)

commit v6 on v5

--- a/solution.py
+++ b/solution.py
@@ -624,14 +624,20 @@
             contract(low, halves, ((1,), (0,))).astype(bf16).reshape(GROUPS, CAP, HALF_WIDE)
         )
 
-    def q_copy(j, d):
+    def q_copy(j, d, part=None):
         target = partner(d)
-        return remote(
-            q_send.at[j, target], q_recv.at[j, me], q_ss.at[j, d], q_rs.at[j, d], (target, seq)
-        )
+        source, goal, sem = q_send.at[j, target], q_recv.at[j, me], j
+        if part is not None:
+            cols = pl.ds(part * (HALF_WIDE // 2), HALF_WIDE // 2)
+            source, goal, sem = source.at[:, cols], goal.at[:, cols], j + part
+        return remote(source, goal, q_ss.at[sem, d], q_rs.at[sem, d], (target, seq))
 
     def start_queries(j):
-        far_first(lambda d: q_copy(j, d).start())
+        if j < HK - 1:
+            far_first(lambda d: q_copy(j, d).start())
+        else:
+            for part in range(2):
+                far_first(lambda d, part=part: q_copy(j, d, part).start())
         q_recv[j, me] = q_send[j, me]
 
     query = seq * TOK + lax.broadcasted_iota(jnp.int32, (TOK, SPAN), 0)
@@ -780,6 +786,8 @@
         def _(d):
             kv_copy(n, d).wait_recv()
 
+    ring_turn(2)
+    start_queries(0)
     pairs_came(0)
     marks_in = kva_recv[:, :, PIECE:].astype(f32)
     column = lax.broadcasted_iota(jnp.int32, (GROUPS, CAP, TOK), 2).astype(f32) + 1.0
@@ -792,8 +800,6 @@
         flag_x_copy(d).start()
     put_low = both_halves(match[:, :LOW]).T.astype(bf16)
 
-    ring_turn(2)
-    start_queries(0)
     forward(0, 2)
     one_back(0)
     ring_turn(3)
@@ -838,50 +844,56 @@
         def _():
             each_x(n, 0, came_x, (2,))
 
-    @pl.loop(0, HK)
-    def _(j):
-        @pl.when(j == 0)
-        def _():
-            window_came(0)
-
-        @pl.when(j == 1)
-        def _():
-            forward(1, 1)
-            forward(1, 0)
-
-        @pl.when(j == 2)
-        def _():
-            window_came(1)
-
-        @pl.loop(1, GROUPS)
-        def _(d):
-            q_copy(j, d).wait_recv()
-
-        cols = pl.ds(pl.multiple_of(j * HALF_WIDE, HALF_WIDE), HALF_WIDE)
-        rows = contract(put_low, q_recv[j].reshape(SLOTS, HALF_WIDE), ((1,), (0,)))
-        rows = rows + contract(put_over, over[:, :, cols].reshape(SLOTS, HALF_WIDE), ((1,), (0,)))
+    def place_queries(j, cols, over_cols):
+        rows = contract(put_low, q_recv[j, :, :, cols].reshape(SLOTS, -1), ((1,), (0,)))
+        rows = rows + contract(put_over, over[:, :, over_cols].reshape(SLOTS, -1), ((1,), (0,)))
         rows = rows.astype(bf16)
-        for h in range(HQ // HK):
-            half, at = h // (HQ // HK // 2), h % (HQ // HK // 2)
-            placed[h] = rows[half * TOK : (half + 1) * TOK, at * HD : (at + 1) * HD]
+        count = rows.shape[1] // HD
+        for n in range(2 * count):
+            half, at = n // count, n % count
+            placed[n] = rows[half * TOK : (half + 1) * TOK, at * HD : (at + 1) * HD]
+
+    def attend(j, heads):
         key_cols = pl.ds(pl.multiple_of(j % 2 * HD, HD), HD)
         value_cols = pl.ds(pl.multiple_of(PIECE // 2 + j % 2 * HD, HD), HD)
-        for h in range(HQ // HK):
+        for n, h in enumerate(heads):
             keys = window[j // 2, pl.ds(x, BACK + 1), :, key_cols].reshape(SPAN, HD)
             values = window[j // 2, pl.ds(x, BACK + 1), :, value_cols].reshape(SPAN, HD)
-            scores = contract(placed[h], keys, ((1,), (1,))) + mask[...]
+            scores = contract(placed[n], keys, ((1,), (1,))) + mask[...]
             top = jnp.max(scores, axis=1, keepdims=True)
             weights = jnp.exp2((scores - top) * FACTOR).astype(bf16)
             summed = contract(weights, jnp.concatenate([values, ones], axis=1), ((1,), (0,)))
             head_cols = pl.ds(pl.multiple_of((j * (HQ // HK) + h) * HD, HD), HD)
             out_ref[0, :, head_cols] = (summed[:, :HD] / summed[:, HD:]).astype(bf16)
 
+    @pl.loop(0, HK - 1)
+    def _(j):
+        @pl.when(j == 0)
+        def _():
+            window_came(0)
+
+        @pl.when(j == 1)
+        def _():
+            forward(1, 1)
+            forward(1, 0)
+
+        @pl.when(j == 2)
+        def _():
+            window_came(1)
+
+        @pl.loop(1, GROUPS)
+        def _(d):
+            q_copy(j, d).wait_recv()
+
+        cols = pl.ds(pl.multiple_of(j * HALF_WIDE, HALF_WIDE), HALF_WIDE)
+        place_queries(j, slice(None), cols)
+        attend(j, range(HQ // HK))
 
     @pl.loop(1, GROUPS)
     def _(d):
         for n in range(2):
             kv_copy(n, d).wait_send()
-        for j in range(HK):
+        for j in range(HK - 1):
             q_copy(j, d).wait_send()
 
     for n in range(2):
@@ -916,6 +928,19 @@
         flag_x_copy(d).wait_send()
     for d in range(1, NZ):
         flag_z_copy(d).wait_send()
+
+    last = HK - 1
+    quarter = HQ // HK // 4
+    for part in range(2):
+
+        @pl.loop(1, GROUPS)
+        def _(d, part=part):
+            q_copy(last, d, part).wait()
+
+        at = part * HALF_WIDE // 2
+        start = last * HALF_WIDE + at
+        place_queries(last, slice(at, at + HALF_WIDE // 2), slice(start, start + HALF_WIDE // 2))
+        attend(last, [2 * quarter * half + part * quarter + n for half in range(2) for n in range(quarter)])
 
 
 def compact(*operands):
@@ -949,8 +974,8 @@
             vmem((NX, CAP, TOK), bf16),
             vmem((NZ, CAP, TOK), bf16),
             dma((2 * HK + 4,)),
-            dma((HK, GROUPS)),
-            dma((HK, GROUPS)),
+            dma((HK + 1, GROUPS)),
+            dma((HK + 1, GROUPS)),
             dma((2, GROUPS)),
             dma((2, GROUPS)),
             dma((2, NY // 2 + 1)),

time: 64.1 us -> 65.2 us (1.017)
  the two profiles are of different devices: /device:TPU:1 before, /device:TPU:136 now
where the time goes in v6:
time: 65.2 us; the launch traced here: 65.1 us
  Pallas kernels  63.2 us (97%)
  local copies, waits for them, and re-layouts  0.97 us (1%)
    pallas_call x1, Pallas kernels, compact(): pl.pallas_call(compact_kernel, out_shape=(pltpu.VMEM((1, TOK, HQ * HD), b...  63.2 us

profile of v6, /device:TPU:136, one launch (start us, length us, event | category | flops | bytes accessed | tf_op | source)
XLA Modules:
  0.0 65.1 jit_solution(4561520150199436646)
XLA Ops:
  0.0 63.2 %shard_map.57 = (bf16[1,128,4096]{2,1,0:T(8,128)(2,1)S(1)}, s32[1,1]{1,0:T(1,128)}) custom-call(bf16[1,128,4096]{2,1,0:T(8,128)(2,1)} %q_hbm.1, bf16[1,128,1024]{2,1,0:T(8,128)(2,1)} %kv_hbm.1, s32[1,128]{1,0:T(1,128)} %group_hbm.1, s32[1,128]{1,0:T(1,128)} %slot_hbm.1, s32[1,2,3]{2,1,0:T(2,128)} %length_hbm.1), custom_call_target="tpu_custom_call" | custom-call | tf_op jit(solution)/shard_map/pallas_call | solution.py:950
  63.9 0.2 conditional.1
  64.1 1.0 %copy.11 = bf16[1,128,4096]{2,1,0:T(8,128)(2,1)} copy(bf16[1,128,4096]{2,1,0:T(8,128)(2,1)S(1)} %get-tuple-element.28) | data formatting | bytes 2097152

commit v7 on v6

--- a/solution.py
+++ b/solution.py
@@ -545,6 +545,61 @@
 
     pack_pairs(0)
 
+    turn = 1 - 2 * core
+
+    def on_ring(at):
+        return (at + 2 * NY) % NY * 2 + core
+
+    def on_sibling(at):
+        return (at + 2 * NY) % NY * 2 + 1 - core
+
+    def ring(step, way):
+        sign = turn if way == 0 else -turn
+        block = on_ring(y - sign * (step - 1))
+        return remote(
+            over.at[block],
+            over.at[block],
+            ring_ss.at[way, step],
+            ring_rs.at[way, step],
+            (on_ring(y + sign), seq),
+        )
+
+    def ring_came(step, way):
+        sign = turn if way == 0 else -turn
+        block = on_ring(y - sign * step)
+        remote(
+            over.at[block],
+            over.at[block],
+            ring_ss.at[way, step],
+            ring_rs.at[way, step],
+            (on_ring(y + sign), seq),
+        ).wait_recv()
+
+    def sibling(n):
+        block = on_ring(y - turn * n if n <= NY // 2 else y + turn * (n - NY // 2))
+        return remote(
+            over.at[block], over.at[block], sib_ss.at[n], sib_rs.at[n], (on_sibling(y), seq)
+        )
+
+    def sibling_came(n):
+        block = on_sibling(y + turn * n if n <= NY // 2 else y - turn * (n - NY // 2))
+        remote(
+            over.at[block], over.at[block], sib_ss.at[n], sib_rs.at[n], (on_sibling(y), seq)
+        ).wait_recv()
+
+    def ring_turn(step):
+        ring_came(step, 0)
+        if step < NY // 2:
+            ring(step + 1, 0).start()
+            ring_came(step, 1)
+            if step + 1 < NY // 2:
+                ring(step + 1, 1).start()
+            sibling(NY // 2 + step).start()
+        sibling(step).start()
+
+    pl.semaphore_wait(barrier, GROUPS - 1 + NX - 1 + NZ - 1)
+    start_pairs(0)
+
     high = both_halves(extra[None]).astype(bf16)
     for j in range(HK):
         loads[2 * j].wait()
@@ -555,67 +610,11 @@
         ).astype(bf16)
     tags = jnp.concatenate([extra * places, extra * (targets + 1).astype(f32)], axis=0)
     over[me, :, HK * HALF_WIDE :] = contract(tags.astype(bf16), all_ones, ((1,), (0,))).astype(bf16)
-    turn = 1 - 2 * core
-
-    def on_ring(at):
-        return (at + 2 * NY) % NY * 2 + core
-
-    def on_sibling(at):
-        return (at + 2 * NY) % NY * 2 + 1 - core
-
-    def ring(step, way):
-        sign = turn if way == 0 else -turn
-        block = on_ring(y - sign * (step - 1))
-        return remote(
-            over.at[block],
-            over.at[block],
-            ring_ss.at[way, step],
-            ring_rs.at[way, step],
-            (on_ring(y + sign), seq),
-        )
-
-    def ring_came(step, way):
-        sign = turn if way == 0 else -turn
-        block = on_ring(y - sign * step)
-        remote(
-            over.at[block],
-            over.at[block],
-            ring_ss.at[way, step],
-            ring_rs.at[way, step],
-            (on_ring(y + sign), seq),
-        ).wait_recv()
-
-    def sibling(n):
-        block = on_ring(y - turn * n if n <= NY // 2 else y + turn * (n - NY // 2))
-        return remote(
-            over.at[block], over.at[block], sib_ss.at[n], sib_rs.at[n], (on_sibling(y), seq)
-        )
-
-    def sibling_came(n):
-        block = on_sibling(y + turn * n if n <= NY // 2 else y - turn * (n - NY // 2))
-        remote(
-            over.at[block], over.at[block], sib_ss.at[n], sib_rs.at[n], (on_sibling(y), seq)
-        ).wait_recv()
-
-    def ring_turn(step):
-        ring_came(step, 0)
-        if step < NY // 2:
-            ring(step + 1, 0).start()
-            ring_came(step, 1)
-            if step + 1 < NY // 2:
-                ring(step + 1, 1).start()
-            sibling(NY // 2 + step).start()
-        sibling(step).start()
-
-    pl.semaphore_wait(barrier, GROUPS - 1 + NX - 1 + NZ - 1)
     ring(1, 0).start()
     ring(1, 1).start()
-    start_pairs(0)
+    pack_pairs(1)
+    start_pairs(1)
     sibling(0).start()
-    pack_pairs(1)
-
-    ring_turn(1)
-    start_pairs(1)
 
     low = both_halves(pick_three[:, :LOW]).astype(bf16)
     for j in range(HK):
@@ -786,8 +785,6 @@
         def _(d):
             kv_copy(n, d).wait_recv()
 
-    ring_turn(2)
-    start_queries(0)
     pairs_came(0)
     marks_in = kva_recv[:, :, PIECE:].astype(f32)
     column = lax.broadcasted_iota(jnp.int32, (GROUPS, CAP, TOK), 2).astype(f32) + 1.0
@@ -800,29 +797,29 @@
         flag_x_copy(d).start()
     put_low = both_halves(match[:, :LOW]).T.astype(bf16)
 
+    ring_turn(1)
+    start_queries(0)
     forward(0, 2)
     one_back(0)
-    ring_turn(3)
-    start_queries(1)
     pairs_came(1)
     place_pairs(1)
+    ring_turn(2)
+    start_queries(1)
     for d in range(1, NX):
         flag_x_copy(d, True).wait_recv()
     flag_z[z] = jnp.max(flag_x[...].astype(f32), axis=0).astype(bf16)
     for d in range(1, NZ):
         flag_z_copy(d).start()
     two_back(0)
-    start_queries(2)
     forward(0, 1)
     one_back(1)
     forward(1, 2)
+    ring_turn(3)
+    start_queries(2)
     start_queries(3)
-    ring_turn(4)
     two_back(1)
     forward(0, 0)
-    for d in range(1, NZ):
-        flag_z_copy(d, True).wait_recv()
-    flag_ref[0, 0] = jnp.max(flag_z[...].astype(f32)).astype(jnp.int32)
+    ring_turn(4)
     for n in range(NY):
         sibling_came(n)
 
@@ -928,6 +925,10 @@
         flag_x_copy(d).wait_send()
     for d in range(1, NZ):
         flag_z_copy(d).wait_send()
+
+    for d in range(1, NZ):
+        flag_z_copy(d, True).wait_recv()
+    flag_ref[0, 0] = jnp.max(flag_z[...].astype(f32)).astype(jnp.int32)
 
     last = HK - 1
     quarter = HQ // HK // 4

time: 65.2 us -> 67.4 us (1.034)
  the two profiles are of different devices: /device:TPU:136 before, /device:TPU:1 now
where the time goes in v7:
time: 67.4 us; the launch traced here: 66.1 us
  Pallas kernels  64.3 us (95%)
  local copies, waits for them, and re-layouts  0.97 us (1%)
    pallas_call x1, Pallas kernels, compact(): pl.pallas_call(compact_kernel, out_shape=(pltpu.VMEM((1, TOK, HQ * HD), b...  64.3 us

profile of v7, /device:TPU:1, one launch (start us, length us, event | category | flops | bytes accessed | tf_op | source)
XLA Modules:
  0.0 66.1 jit_solution(1361162414910049336)
XLA Ops:
  0.0 64.3 %shard_map.57 = (bf16[1,128,4096]{2,1,0:T(8,128)(2,1)S(1)}, s32[1,1]{1,0:T(1,128)}) custom-call(bf16[1,128,4096]{2,1,0:T(8,128)(2,1)} %q_hbm.1, bf16[1,128,1024]{2,1,0:T(8,128)(2,1)} %kv_hbm.1, s32[1,128]{1,0:T(1,128)} %group_hbm.1, s32[1,128]{1,0:T(1,128)} %slot_hbm.1, s32[1,2,3]{2,1,0:T(2,128)} %length_hbm.1), custom_call_target="tpu_custom_call" | custom-call | tf_op jit(solution)/shard_map/pallas_call | solution.py:951
  64.9 0.2 conditional.1
  65.1 1.0 %copy.11 = bf16[1,128,4096]{2,1,0:T(8,128)(2,1)} copy(bf16[1,128,4096]{2,1,0:T(8,128)(2,1)S(1)} %get-tuple-element.28) | data formatting | bytes 2097152

commit v8 on v5

--- a/solution.py
+++ b/solution.py
@@ -814,9 +814,6 @@
     ring_turn(4)
     two_back(1)
     forward(0, 0)
-    for d in range(1, NZ):
-        flag_z_copy(d, True).wait_recv()
-    flag_ref[0, 0] = jnp.max(flag_z[...].astype(f32)).astype(jnp.int32)
     for n in range(NY):
         sibling_came(n)
 
@@ -876,6 +873,10 @@
             head_cols = pl.ds(pl.multiple_of((j * (HQ // HK) + h) * HD, HD), HD)
             out_ref[0, :, head_cols] = (summed[:, :HD] / summed[:, HD:]).astype(bf16)
 
+
+    for d in range(1, NZ):
+        flag_z_copy(d, True).wait_recv()
+    flag_ref[0, 0] = jnp.max(flag_z[...].astype(f32)).astype(jnp.int32)
 
     @pl.loop(1, GROUPS)
     def _(d):

time: 64.1 us -> 64.2 us (level)
  no operation moved by 1% of the time
where the time goes in v8:
time: 64.2 us; the launch traced here: 63.5 us
  Pallas kernels  61.9 us (96%)
  local copies, waits for them, and re-layouts  0.97 us (2%)
  between operations  0.65 us (1%)
    pallas_call x1, Pallas kernels, compact(): pl.pallas_call(compact_kernel, out_shape=(pltpu.VMEM((1, TOK, HQ * HD), b...  61.9 us

profile of v8, /device:TPU:1, one launch (start us, length us, event | category | flops | bytes accessed | tf_op | source)
XLA Modules:
  0.0 63.5 jit_solution(8454910454293844028)
XLA Ops:
  0.0 61.9 %shard_map.57 = (bf16[1,128,4096]{2,1,0:T(8,128)(2,1)S(1)}, s32[1,1]{1,0:T(1,128)}) custom-call(bf16[1,128,4096]{2,1,0:T(8,128)(2,1)} %q_hbm.1, bf16[1,128,1024]{2,1,0:T(8,128)(2,1)} %kv_hbm.1, s32[1,128]{1,0:T(1,128)} %group_hbm.1, s32[1,128]{1,0:T(1,128)} %slot_hbm.1, s32[1,2,3]{2,1,0:T(2,128)} %length_hbm.1), custom_call_target="tpu_custom_call" | custom-call | tf_op jit(solution)/shard_map/pallas_call | solution.py:926
  62.5 1.0 %copy.11 = bf16[1,128,4096]{2,1,0:T(8,128)(2,1)} copy(bf16[1,128,4096]{2,1,0:T(8,128)(2,1)S(1)} %get-tuple-element.28) | data formatting | bytes 2097152
  (1 shorter events, 0.0 us)
